TPU v7x, 32 devices: a whole 2x2x4 slice. The times are simulated.
32 devices in a mesh: row: 4 (over y, core), col: 8 (over z, x).
Axes of the slice: x: 2, y: 2, z: 4, core: 2. Of those that a mesh axis runs over, the one named last changes fastest.
Arguments:
- prior_solved: bfloat16 [92160, 768], P('col'), may hold values from -6 to 6
- lower_prior: bfloat16 [92160, 2, 3072], P('col', None, 'row'), may hold values from -0.01953125 to 0.01953125
- rhs: bfloat16 [2, 3072, 768], P(None, 'row'), may hold values from -6 to 6
- coupling: bfloat16 [3072, 3072], P('col', 'row'), may hold values from -0.109375 to 0.109375
- inverse_diag: bfloat16 [2, 3072, 3072], P(None, 'col', 'row'), may hold values from -1 to 1, as said below
Outputs:
- solved: bfloat16 [2, 3072, 768], P(None, 'row')
Inputs may be any that keep to these rules, and one draw needn't show every extreme that they name: Each block inverse_diag[b] is the inverse of a unit lower triangular block: entry [b, j, i] is zero for j > i and exactly one for j == i.
All inputs are finite; a program needn't handle non-finite values.
Results may differ from a plain program's by a relative error of at most 0.0056.
Values may be sent and summed in bfloat16 or wider, within the bound.
A program may use at most 192 MiB of HBM per device.

v0:
```python
import jax
import jax.numpy as jnp
from jax import lax
from jax.sharding import PartitionSpec as P


def local_product(left_block, right_rows):
    return lax.dot_general(
        left_block, right_rows, (((0,), (0,)), ((), ())), preferred_element_type=jnp.float32
    )


def on_device(prior_solved, lower_prior, rhs, coupling, inverse_diag):
    share_width = rhs.shape[2] // lax.axis_size("col")
    share_start = lax.axis_index("col") * share_width
    stacked = jnp.stack([inverse_diag[0], coupling, inverse_diag[1]])
    whole_blocks = lax.all_gather(stacked, "col", axis=1, tiled=True)
    both_terms = jnp.stack(
        [
            local_product(lower_prior[:, 0, :], prior_solved),
            local_product(lower_prior[:, 1, :], prior_solved),
        ]
    )
    shares = lax.psum_scatter(both_terms, "col", scatter_dimension=2, tiled=True)
    rhs_share = lax.dynamic_slice_in_dim(rhs, share_start, share_width, 2).astype(jnp.float32)

    def apply_share(left_block, vector_rows):
        full_vector = lax.all_gather(vector_rows, "row", axis=0, tiled=True)
        return local_product(left_block, full_vector)

    first_reduced = (rhs_share[0] - shares[0]).astype(jnp.bfloat16)
    first_solved = apply_share(whole_blocks[0], first_reduced).astype(jnp.bfloat16)
    cross_term = apply_share(whole_blocks[1], first_solved)
    second_reduced = (rhs_share[1] - shares[1] - cross_term).astype(jnp.bfloat16)
    second_solved = apply_share(whole_blocks[2], second_reduced).astype(jnp.bfloat16)
    solved_share = jnp.stack([first_solved, second_solved])
    return lax.all_gather(solved_share, "col", axis=2, tiled=True)


def solution(mesh):
    return jax.shard_map(
        on_device,
        mesh=mesh,
        in_specs=(
            P("col", None),
            P("col", None, "row"),
            P(None, "row", None),
            P("col", "row"),
            P(None, "col", "row"),
        ),
        out_specs=P(None, "row", None),
        check_vma=False,
    )
```

profile of v0, /device:TPU:0, one launch (start us, length us, event | category | flops | bytes accessed | tf_op | source)
XLA Modules:
  0.0 592.7 jit_solution(14321367190984049942)
XLA Ops:
  6.5 0.0 copy-start
  6.5 0.0 all-reduce.3.cloned.1.call-start
  6.5 67.6 %fusion.15 = (bf16[11520,1,768]{2,1,0:T(2,128)(2,1)}, bf16[11520,1,768]{2,1,0:T(2,128)(2,1)}) fusion(bf16[11520,2,768]{2,1,0:T(2,128)(2,1)} %param.6), kind=kLoop, calls=%fused_computation.28 | loop fusion | bytes 70778880 | tf_op jit(solution)/shard_map/slice | solution.py:20
  74.1 24.8 %fusion.5 = f32[1,768,768]{2,1,0:T(8,128)} fusion(bf16[11520,768]{1,0:T(8,128)(2,1)} %param.5, bf16[11520,1,768]{2,1,0:T(2,128)(2,1)} %get-tuple-element.5), kind=kOutput, calls=%fused_computation.12 | convolution fusion | flops 13589544960 | bytes 37748736 | tf_op jit(solution)/shard_map/dot_general | solution.py:8
  99.0 24.7 %fusion.6 = f32[1,768,768]{2,1,0:T(8,128)} fusion(bf16[11520,768]{1,0:T(8,128)(2,1)} %param.5, bf16[11520,1,768]{2,1,0:T(2,128)(2,1)} %get-tuple-element.6), kind=kOutput, calls=%fused_computation.13 | convolution fusion | flops 13589544960 | bytes 37748736 | tf_op jit(solution)/shard_map/dot_general | solution.py:8
  123.7 4.8 pad_maximum_fusion
  128.5 8.2 %copy.13 = f32[2,768,768]{1,0,2:T(2,128)} copy(f32[2,768,768]{2,1,0:T(8,128)} %pad_maximum_fusion) | data formatting | bytes 9437184 | tf_op jit(solution)/shard_map/stack | solution.py:18
  136.7 0.0 all-reduce.3.cloned.1.call-update
  136.7 0.0 copy-start.3
  136.8 0.0 all-gather.4.cloned.1.call-start
  136.8 1.2 copy-done.1
  138.0 0.1 fusion.16
  138.1 2.5 pad_maximum_fusion.1
  140.5 0.0 all-gather.4.cloned.1.call-update
  140.6 0.2 all-gather.6.cloned.1.call-start
  140.8 0.0 copy-done
  140.8 0.2 constant_dynamic-slice_fusion.2
  141.0 0.2 copy.17
  141.2 0.7 dynamic-slice
  142.6 166.6 %all-reduce.3.cloned.1.call-done = f32[2,768,768]{1,0,2:T(2,128)} async-done(((f32[2,768,768]{1,0,2:T(2,128)}), f32[2,768,768]{1,0,2:T(2,128)}) %all-reduce.3.cloned.1.call-update) | async-done | bytes 4718608
  309.2 2.5 constant_dynamic-slice_fusion.1
  311.7 7.5 %all-gather = bf16[1,3072,96]{1,2,0:T(8,128)(2,1)S(1)} all-gather(bf16[1,768,96]{1,2,0:T(8,128)(2,1)S(1)} %fusion.14), channel_id=2, replica_groups=mesh['row'=4,'col'=8] {'row'}, dimensions={1}, use_global_device_ids=true | all-gather | bytes 737280 | tf_op jit(solution)/shard_map/all_gather | solution.py:28
  319.3 186.8 %all-gather.4.cloned.1.call-done = bf16[3,3072,768]{2,1,0:T(8,128)(2,1)} async-done(((bf16[3,384,768]{2,1,0:T(8,128)(2,1)}), bf16[3,3072,768]{2,1,0:T(8,128)(2,1)}) %all-gather.4.cloned.1.call-update) | async-done | bytes 14155792 | tf_op jit(solution)/shard_map/all_gather | solution.py:17
  506.1 3.3 fusion.8
  509.4 7.5 %all_gather.17 = bf16[3072,96]{0,1:T(8,128)(2,1)S(1)} all-gather(bf16[768,96]{0,1:T(8,128)(2,1)S(1)} %fusion.8), channel_id=1, replica_groups=mesh['row'=4,'col'=8] {'row'}, dimensions={0}, use_global_device_ids=true | all-gather | bytes 737280 | tf_op jit(solution)/shard_map/all_gather | solution.py:28
  516.9 3.2 fusion.10
  520.1 7.7 %all_gather.18 = bf16[3072,96]{0,1:T(8,128)(2,1)S(1)} all-gather(bf16[768,96]{0,1:T(8,128)(2,1)S(1)} %fusion.10), channel_id=1, replica_groups=mesh['row'=4,'col'=8] {'row'}, dimensions={0}, use_global_device_ids=true | all-gather | bytes 737280 | tf_op jit(solution)/shard_map/all_gather | solution.py:28
  527.8 3.2 fusion.11
  531.0 0.7 pad_maximum_fusion.2
  531.7 0.0 all-gather.6.cloned.1.call-update
  531.7 50.2 %all-gather.6.cloned.1.call-done = bf16[2,768,768]{1,2,0:T(8,128)(2,1)} async-done(((bf16[2,768,96]{1,2,0:T(8,128)(2,1)}), bf16[2,768,768]{1,2,0:T(8,128)(2,1)}) %all-gather.6.cloned.1.call-update) | async-done | bytes 2359312 | tf_op jit(solution)/shard_map/all_gather | solution.py:37
  581.9 4.3 copy.16
  (6 shorter events, 0.1 us)
Async XLA Ops:
  6.5 134.3 %copy-start = (bf16[2,768,768]{2,1,0:T(8,128)(2,1)S(1)}, bf16[2,768,768]{2,1,0:T(8,128)(2,1)}, u32[]{:S(2)}) copy-start(bf16[2,768,768]{2,1,0:T(8,128)(2,1)} %param.7) | copy-start | bytes 7077892
  6.5 302.7 %all-reduce.3.cloned.1.call-start = ((), (), s32[]{:S(2)}) async-start(), calls=%async_computation.2 | async-start | bytes 9437184
  136.7 1.3 copy-start.1
  136.7 4.5 copy-start.3
  136.8 369.3 %all-gather.4.cloned.1.call-start = ((), (), s32[]{:S(2)}) async-start(), calls=%async_computation | async-start | bytes 15925248 | tf_op jit(solution)/shard_map/all_gather | solution.py:17
  140.6 441.4 %all-gather.6.cloned.1.call-start = ((), (), s32[]{:S(2)}) async-start(), calls=%async_computation.1 | async-start | bytes 2654208 | tf_op jit(solution)/shard_map/all_gather | solution.py:37
  506.1 10.8 %copy-start.2 = (f32[1,768,96]{1,0,2:T(1,128)S(1)}, f32[1,768,96]{1,0,2:T(1,128)}, u32[]{:S(2)}) copy-start(f32[1,768,96]{1,0,2:T(1,128)} %get-tuple-element.7) | copy-start | bytes 884740
Sparse Core Ops, SparseCore 0:
  136.9 172.3 all-reduce.2
  311.4 194.6 all-gather.3
  531.9 50.0 all-gather.5
where the time goes:
time: 593 us
  waiting for transfers between devices  404 us (68%)
  local copies, waits for them, and re-layouts  84.8 us (14%)
  matrix products  59.3 us (10%)
  blocking collectives  22.7 us (4%)
  between operations  13.9 us (2%)
  other arithmetic  8.09 us (1%)
    all_gather x1, waiting for transfers between devices, on_device(): whole_blocks = lax.all_gather(stacked, 'col', axis=1, tiled=True)  187 us
    unnamed x4, waiting for transfers between devices  167 us
    slice x1, local copies, waits for them, and re-layouts, on_device(): lower_prior[:, 0, :]  67.6 us
    dot_general x5, matrix products, local_product(): lax.dot_general(left_block, right_rows, (((0,), (0,)), ((), ())), preferr...  59.3 us
    all_gather x1, waiting for transfers between devices, on_device(): return lax.all_gather(solved_share, 'col', axis=2, tiled=True)  50.2 us
    all_gather x3, blocking collectives, apply_share(): full_vector = lax.all_gather(vector_rows, 'row', axis=0, tiled=True)  22.7 us
  transfers between devices with their start and end apart: 3, of which 3 were waited for; matrix products, arithmetic and copies ran while one was open for 1% of the time, Pallas kernels for 0%

commit v1 on v0

v1 whole, which is shorter than its diff:
```python
import jax
import jax.numpy as jnp
from jax import lax
from jax.sharding import PartitionSpec as P


def product(left, right, left_dim):
    return lax.dot_general(
        left, right, (((left_dim,), (0,)), ((), ())), preferred_element_type=jnp.float32
    )


def on_device(prior_solved, lower_prior, rhs, coupling, inverse_diag):
    ncol = lax.axis_size("col")
    rows, width = rhs.shape[1], rhs.shape[2]
    share = width // ncol
    share_start = lax.axis_index("col") * share
    first_inverse = lax.all_gather(inverse_diag[0], "col", axis=0, tiled=True)
    whole_coupling = lax.all_gather(coupling, "col", axis=0, tiled=True)
    second_inverse = lax.all_gather(inverse_diag[1], "col", axis=0, tiled=True)
    rhs_share = lax.dynamic_slice_in_dim(rhs, share_start, share, 2).astype(jnp.float32)
    rhs_share = rhs_share.transpose(0, 2, 1)
    terms = product(lower_prior, prior_solved, 0).astype(jnp.bfloat16)
    terms = terms.transpose(2, 0, 1).reshape(ncol, share, 2, rows).transpose(0, 2, 1, 3)
    swapped = lax.all_to_all(terms, "col", 0, 0, tiled=True)
    shares = jnp.sum(swapped.astype(jnp.float32), axis=0)

    def apply_share(vector_rows, left_block):
        full_vector = lax.all_gather(vector_rows, "row", axis=1, tiled=True)
        return product(full_vector, left_block, 1)

    first_reduced = (rhs_share[0] - shares[0]).astype(jnp.bfloat16)
    first_solved = apply_share(first_reduced, first_inverse).astype(jnp.bfloat16)
    cross_term = apply_share(first_solved, whole_coupling)
    second_reduced = (rhs_share[1] - shares[1] - cross_term).astype(jnp.bfloat16)
    second_solved = apply_share(second_reduced, second_inverse).astype(jnp.bfloat16)
    first_out = lax.all_gather(first_solved, "col", axis=0, tiled=True)
    second_out = lax.all_gather(second_solved, "col", axis=0, tiled=True)
    return jnp.stack([first_out.T, second_out.T])


def solution(mesh):
    return jax.shard_map(
        on_device,
        mesh=mesh,
        in_specs=(
            P("col", None),
            P("col", None, "row"),
            P(None, "row", None),
            P("col", "row"),
            P(None, "col", "row"),
        ),
        out_specs=P(None, "row", None),
        check_vma=False,
    )
```

time: 593 us -> 392 us (0.66)
  waiting for transfers between devices: 404 us -> 287 us
  local copies, waits for them, and re-layouts: 84.8 us -> 10.2 us
  matrix products: 59.3 us -> 44.9 us
  starting transfers between devices: 0.27 us -> 7.41 us
    unnamed x4 -> x5, waiting for transfers between devices: 167 us -> 1.94 us
    all_to_all x0 -> x1, waiting for transfers between devices: none -> 84.3 us  [on_device(): swapped = lax.all_to_all(terms, 'col', 0, 0, tiled=True)]
    slice x3 -> x1, local copies, waits for them, and re-layouts: 70.2 us -> 2.49 us  [on_device(): second_inverse = lax.all_gather(inverse_diag[1], 'col', axis=0, tiled=True)]
    all_gather x2 -> x5, waiting for transfers between devices: 237 us -> 200 us  [the longest x1 69.5 us: on_device(): second_inverse = lax.all_gather(inverse_diag[1], 'col', axis=0, tiled=True)]
    dot_general x5 -> x4, matrix products: 59.3 us -> 44.9 us  [product(): lax.dot_general(left, right, (((left_dim,), (0,)), ((), ())), preferred_e...]
    all_to_all x0 -> x1, starting transfers between devices: none -> 7.25 us  [on_device(): swapped = lax.all_to_all(terms, 'col', 0, 0, tiled=True)]
  transfers between devices with their start and end apart: 3 -> 6, of which waited for: 3 -> 5; matrix products, arithmetic and copies ran while one was open for 1% -> 12% of each run, Pallas kernels for 0% -> 0%
where the time goes in v1:
time: 392 us
  waiting for transfers between devices  287 us (73%)
  matrix products  44.9 us (11%)
  blocking collectives  22.9 us (6%)
  between operations  13.2 us (3%)
  local copies, waits for them, and re-layouts  10.2 us (3%)
  starting transfers between devices  7.41 us (2%)
  other arithmetic  6.52 us (2%)
    all_to_all x1, waiting for transfers between devices, on_device(): swapped = lax.all_to_all(terms, 'col', 0, 0, tiled=True)  84.3 us
    all_gather x1, waiting for transfers between devices, on_device(): second_inverse = lax.all_gather(inverse_diag[1], 'col', axis=0, tiled=True)  69.5 us
    all_gather x1, waiting for transfers between devices, on_device(): whole_coupling = lax.all_gather(coupling, 'col', axis=0, tiled=True)  50.3 us
    dot_general x4, matrix products, product(): lax.dot_general(left, right, (((left_dim,), (0,)), ((), ())), preferred_e...  44.9 us
    all_gather x1, waiting for transfers between devices, on_device(): first_out = lax.all_gather(first_solved, 'col', axis=0, tiled=True)  41.9 us
    all_gather x1, waiting for transfers between devices, on_device(): second_out = lax.all_gather(second_solved, 'col', axis=0, tiled=True)  38.8 us
    all_gather x3, blocking collectives, apply_share(): full_vector = lax.all_gather(vector_rows, 'row', axis=1, tiled=True)  22.9 us
  transfers between devices with their start and end apart: 6, of which 5 were waited for; matrix products, arithmetic and copies ran while one was open for 12% of the time, Pallas kernels for 0%

profile of v1, /device:TPU:0, one launch (start us, length us, event | category | flops | bytes accessed | tf_op | source)
XLA Modules:
  0.0 391.8 jit_solution(4894113167068976436)
XLA Ops:
  6.5 2.5 fusion.22
  9.0 0.0 all-gather.15.cloned.1.call-update
  9.1 0.0 all-gather.11.cloned.1.call-start
  9.1 0.7 all-gather.11.cloned.1.call-update
  9.8 0.0 all-gather.17.cloned.1.call-start
  9.8 0.7 all-gather.17.cloned.1.call-update
  10.5 33.9 %fusion.7 = bf16[768,2,768]{2,0,1:T(8,128)(2,1)S(1)} fusion(bf16[11520,2,768]{2,1,0:T(2,128)(2,1)} %param.6, bf16[11520,768]{1,0:T(8,128)(2,1)} %param.5), kind=kOutput, calls=%fused_computation.10 | convolution fusion | flops 27180269568 | bytes 55443456 | tf_op jit(solution)/shard_map/dot_general | solution.py:8
  44.4 1.6 copy.26
  46.0 7.3 %all-to-all-start = ((bf16[8,2,96,768]{3,2,1,0:T(8,128)(2,1)}), bf16[8,2,96,768]{3,2,1,0:T(8,128)(2,1)}, u32[]{:S(2)}, u32[]{:S(2)}) async-start(bf16[8,2,96,768]{3,2,1,0:T(8,128)(2,1)} %bitcast.37), calls=%async_computation | async-start | bytes 4718592 | tf_op jit(solution)/shard_map/all_to_all | solution.py:25
  53.3 0.0 all-gather.13.cloned.1.call-start
  53.3 0.2 constant_dynamic-slice_fusion
  53.5 0.9 copy.18
  54.4 1.0 convert_bitcast_fusion
  55.4 84.3 %all-to-all-done = bf16[8,2,96,768]{3,2,1,0:T(8,128)(2,1)} async-done(((bf16[8,2,96,768]{3,2,1,0:T(8,128)(2,1)}), bf16[8,2,96,768]{3,2,1,0:T(8,128)(2,1)}, u32[]{:S(2)}, u32[]{:S(2)}) %all-to-all-start) | async-done | bytes 2359328 | tf_op jit(solution)/shard_map/all_to_all | solution.py:25
  139.7 2.2 convert_reduce_fusion
  141.9 0.0 copy-start.1
  142.0 0.8 copy-done.1
  142.8 7.6 %all-gather = bf16[1,96,3072]{2,1,0:T(8,128)(2,1)S(1)} all-gather(bf16[1,96,768]{2,1,0:T(8,128)(2,1)S(1)} %fusion.21), channel_id=2, replica_groups=mesh['row'=4,'col'=8] {'row'}, dimensions={2}, use_global_device_ids=true | all-gather | bytes 737280 | tf_op jit(solution)/shard_map/all_gather | solution.py:29
  150.4 3.9 fusion.12
  154.3 7.8 %all_gather.27 = bf16[96,3072]{1,0:T(8,128)(2,1)S(1)} all-gather(bf16[96,768]{1,0:T(8,128)(2,1)} %fusion.12), channel_id=1, replica_groups=mesh['row'=4,'col'=8] {'row'}, dimensions={1}, use_global_device_ids=true | all-gather | bytes 737280 | tf_op jit(solution)/shard_map/all_gather | solution.py:29
  162.1 50.3 %all-gather.11.cloned.1.call-done = bf16[3072,768]{1,0:T(8,128)(2,1)} async-done(((bf16[384,768]{1,0:T(8,128)(2,1)}), bf16[3072,768]{1,0:T(8,128)(2,1)}) %all-gather.11.cloned.1.call-update) | async-done | bytes 4718608 | tf_op jit(solution)/shard_map/all_gather | solution.py:19
  212.4 3.3 fusion.18
  215.6 7.5 %all_gather.29 = bf16[96,3072]{1,0:T(8,128)(2,1)S(1)} all-gather(bf16[96,768]{1,0:T(8,128)(2,1)S(1)} %fusion.18), channel_id=1, replica_groups=mesh['row'=4,'col'=8] {'row'}, dimensions={1}, use_global_device_ids=true | all-gather | bytes 737280 | tf_op jit(solution)/shard_map/all_gather | solution.py:29
  223.1 69.5 %all-gather.17.cloned.1.call-done = bf16[1,3072,768]{2,1,0:T(8,128)(2,1)} async-done(((bf16[1,384,768]{2,1,0:T(8,128)(2,1)}), bf16[1,3072,768]{2,1,0:T(8,128)(2,1)}) %all-gather.17.cloned.1.call-update) | async-done | bytes 4718608 | tf_op jit(solution)/shard_map/all_gather | solution.py:20
  292.6 3.9 fusion.15
  296.5 0.0 all-gather.13.cloned.1.call-update
  296.5 0.0 all-gather.9.cloned.1.call-start
  296.6 0.5 all-gather.9.cloned.1.call-update
  297.1 38.8 %all-gather.13.cloned.1.call-done = bf16[768,768]{1,0:T(8,128)(2,1)} async-done(((bf16[96,768]{1,0:T(8,128)(2,1)}), bf16[768,768]{1,0:T(8,128)(2,1)}) %all-gather.13.cloned.1.call-update) | async-done | bytes 1179664 | tf_op jit(solution)/shard_map/all_gather | solution.py:38
  335.9 41.9 %all-gather.9.cloned.1.call-done = bf16[768,768]{1,0:T(8,128)(2,1)} async-done(((bf16[96,768]{1,0:T(8,128)(2,1)}), bf16[768,768]{1,0:T(8,128)(2,1)}) %all-gather.9.cloned.1.call-update) | async-done | bytes 1179664 | tf_op jit(solution)/shard_map/all_gather | solution.py:37
  377.8 3.3 pad_maximum_fusion
  381.0 4.3 %copy.14 = bf16[2,768,768]{2,1,0:T(8,128)(2,1)} copy(bf16[2,768,768]{1,2,0:T(8,128)(2,1)} %pad_maximum_fusion) | data formatting | bytes 4718592 | tf_op jit(solution)/shard_map/stack | solution.py:39
  (5 shorter events, 0.0 us)
Async XLA Ops:
  6.5 46.8 %copy-start = (bf16[2,768,768]{2,1,0:T(8,128)(2,1)S(1)}, bf16[2,768,768]{2,1,0:T(8,128)(2,1)}, u32[]{:S(2)}) copy-start(bf16[2,768,768]{2,1,0:T(8,128)(2,1)} %param.7) | copy-start | bytes 7077892
  6.5 143.8 %all-gather.15.cloned.1.call-start = ((), (), s32[]{:S(2)}) async-start(), calls=%async_computation.4 | async-start | bytes 5308416 | tf_op jit(solution)/shard_map/all_gather | solution.py:18
  9.1 203.3 %all-gather.11.cloned.1.call-start = ((), (), s32[]{:S(2)}) async-start(), calls=%async_computation.2 | async-start | bytes 5308416 | tf_op jit(solution)/shard_map/all_gather | solution.py:19
  9.8 282.8 %all-gather.17.cloned.1.call-start = ((), (), s32[]{:S(2)}) async-start(), calls=%async_computation.5 | async-start | bytes 5308416 | tf_op jit(solution)/shard_map/all_gather | solution.py:20
  46.0 93.7 %all-to-all-start = ((bf16[8,2,96,768]{3,2,1,0:T(8,128)(2,1)}), bf16[8,2,96,768]{3,2,1,0:T(8,128)(2,1)}, u32[]{:S(2)}, u32[]{:S(2)}) async-start(bf16[8,2,96,768]{3,2,1,0:T(8,128)(2,1)} %bitcast.37), calls=%async_computation | async-start | bytes 4718592 | tf_op jit(solution)/shard_map/all_to_all | solution.py:25
  53.3 282.6 %all-gather.13.cloned.1.call-start = ((), (), s32[]{:S(2)}) async-start(), calls=%async_computation.3 | async-start | bytes 1327104 | tf_op jit(solution)/shard_map/all_gather | solution.py:38
  141.9 0.8 copy-start.1
  296.5 81.2 %all-gather.9.cloned.1.call-start = ((), (), s32[]{:S(2)}) async-start(), calls=%async_computation.1 | async-start | bytes 1327104 | tf_op jit(solution)/shard_map/all_gather | solution.py:37
Sparse Core Ops, SparseCore 0:
  9.5 121.6 all-gather.14
  133.4 78.9 all-gather.10
  214.6 78.0 all-gather.16
  296.6 39.1 all-gather.12
  337.9 39.8 all-gather.8
